TPU v7x, 32 devices: a whole 2x2x4 slice. The times are simulated.
32 devices in a mesh: freq: 8 (over z, x), space: 4 (over y, core).
Axes of the slice: x: 2, y: 2, z: 4, core: 2. Of those that a mesh axis runs over, the one named last changes fastest.
Arguments:
- record: float32 [512, 3, 16384], P('freq', None, 'space'), may hold values from -6 to 6
- area_weight: float32 [16384], P('space'), may hold values from 0.2 to 5
- freq_bins: int32 [8], replicated, may hold values from 0 to 64, as said below
Outputs:
- modes: bfloat16 [8, 8, 2, 3, 16384], P('freq', None, None, None, 'space')
- factor: float32 [8, 2, 8, 8], P('freq')
Inputs may be any that keep to these rules, and one draw needn't show every extreme that they name: `freq_bins`: the bins are distinct; bin 0 and bin 128 / 2 are always among them.
All inputs are finite; a program needn't handle non-finite values.
Results may differ from a plain program's by a relative error of at most 0.001.
Values sent between devices are 32-bit elements; how exact they have to be, the bound alone decides.
A program may use at most 128 MiB of HBM per device.

v0:
```python
import math

import jax
import jax.numpy as jnp
from jax import lax
from jax.sharding import PartitionSpec as P

PTS = 16384
SAMPLES = 128


def shifted(value, axis, steps):
    count = lax.axis_size(axis)
    pairs = [(source, (source + steps) % count) for source in range(count)]
    return lax.ppermute(value, axis, pairs)


def spectral_table(freq_bins):
    sample_index = jnp.arange(SAMPLES, dtype=jnp.int32)
    phase_steps = freq_bins[:, None] * sample_index[None, :] % SAMPLES
    angles = phase_steps.astype(jnp.float32) * (2.0 * math.pi / SAMPLES)
    window = 0.5 - 0.5 * jnp.cos(sample_index.astype(jnp.float32) * (2.0 * math.pi / SAMPLES))
    window = window / jnp.sqrt(jnp.sum(window * window))
    return jnp.stack([jnp.cos(angles), -jnp.sin(angles)], axis=1) * window


def complex_form(partial_value):
    bin_count = partial_value.shape[0]
    half_size = partial_value.shape[1] // 2
    blocked = partial_value.reshape(bin_count, half_size, 2, half_size, 2)
    real_part = blocked[:, :, 0, :, 0] + blocked[:, :, 1, :, 1]
    imag_part = blocked[:, :, 0, :, 1] - blocked[:, :, 1, :, 0]
    upper_rows = jnp.stack([real_part, imag_part], axis=-1)
    lower_rows = jnp.stack([-imag_part, real_part], axis=-1)
    assembled = jnp.stack([upper_rows, lower_rows], axis=2)
    return assembled.reshape(bin_count, 2 * half_size, 2 * half_size)


def apply_table(transform, groups):
    return jnp.einsum("fqn,bncp->fbqcp", transform, groups, precision=lax.Precision.HIGHEST)


def per_device(record, area_weight, freq_bins):
    transform = spectral_table(freq_bins)
    half_len = SAMPLES // 2
    slab_len = record.shape[0]
    groups = record.reshape(slab_len // half_len, half_len, record.shape[1], record.shape[2])
    following = shifted(record, "freq", -1)
    later_groups = jnp.concatenate([record[half_len:], following], axis=0).reshape(groups.shape)
    spectra = apply_table(transform[:, :, :half_len], groups) + apply_table(
        transform[:, :, half_len:], later_groups
    )
    regrouped = lax.all_to_all(spectra, "freq", split_axis=0, concat_axis=1, tiled=True)
    bin_count = regrouped.shape[0]
    block_count = regrouped.shape[1]
    row_count = regrouped.shape[3] * regrouped.shape[4]
    flattened = regrouped.reshape(bin_count, 2 * block_count, row_count)
    weighted = (regrouped * (area_weight / (3 * PTS))).reshape(
        bin_count, 2 * block_count, row_count
    )
    partial_value = jnp.einsum("fir,fjr->fij", weighted, flattened, precision=lax.Precision.HIGHEST)
    local_gram = complex_form(partial_value)
    lower_factor = jnp.linalg.cholesky(lax.psum(local_gram, "space"))
    solved = lax.linalg.triangular_solve(lower_factor, flattened, left_side=True, lower=True)
    modes = solved.reshape(regrouped.shape).astype(jnp.bfloat16)
    upper_blocks = jnp.swapaxes(lower_factor, 1, 2).reshape(
        bin_count, block_count, 2, block_count, 2
    )
    factor = jnp.stack([upper_blocks[:, :, 0, :, 0], upper_blocks[:, :, 0, :, 1]], axis=1)
    return (modes, factor)


def solution(mesh):
    return jax.shard_map(
        per_device,
        mesh=mesh,
        in_specs=(P("freq", None, "space"), P("space"), P()),
        out_specs=(P("freq", None, None, None, "space"), P("freq", None, None, None)),
        check_vma=False,
    )
```

profile of v0, /device:TPU:0, one launch (start us, length us, event | category | flops | bytes accessed | tf_op | source)
XLA Modules:
  0.0 122.8 jit_solution(16910994316252789507)
XLA Ops:
  0.6 6.0 %collective-permute-start = (f32[64,3,4096]{2,0,1:T(8,128)}, f32[64,3,4096]{2,0,1:T(8,128)S(1)}, u32[]{:S(2)}, u32[]{:S(2)}) collective-permute-start(f32[64,3,4096]{2,0,1:T(8,128)} %param.3), channel_id=1, source_target_pairs={{0,28},{4,0},{8,4},{12,8},{16,12},{20,16},{24,20},{28,24},{1,29},{... | collective-permute-start | bytes 9437192 | tf_op jit(solution)/shard_map/ppermute | solution.py:15
  6.7 0.6 multiply_reduce_fusion
  8.0 0.8 fusion.20
  8.8 3.5 %fusion.3 = f32[8,2,3,4096]{3,0,2,1:T(8,128)S(1)} fusion(f32[64,3,4096]{2,0,1:T(8,128)} %param.3, f32[8,2,128]{2,0,1:T(8,128)S(1)} %maximum_multiply_fusion), kind=kOutput, calls=%fused_computation.5 | convolution fusion | flops 150994944 | bytes 3940352 | tf_op jit(solution)/shard_map/fqn,bncp->fbqcp/dot_general | solution.py:40
  12.3 0.0 copy-start
  12.3 62.0 %collective-permute-done = f32[64,3,4096]{2,0,1:T(8,128)S(1)} collective-permute-done((f32[64,3,4096]{2,0,1:T(8,128)}, f32[64,3,4096]{2,0,1:T(8,128)S(1)}, u32[]{:S(2)}, u32[]{:S(2)}) %collective-permute-start) | collective-permute-done | bytes 3145760 | tf_op jit(solution)/shard_map/ppermute | solution.py:15
  74.3 1.6 %fusion = f32[8,1,2,3,4096]{4,0,3,2,1:T(8,128)S(1)} fusion(f32[8,2,3,4096]{3,0,2,1:T(8,128)S(1)} %fusion.3, f32[64,3,4096]{2,0,1:T(8,128)S(1)} %collective-permute-done, f32[8,2,128]{2,0,1:T(8,128)S(1)} %maximum_multiply_fusion), kind=kOutput, calls=%fused_computation.1 | convolution fusion | flops 151191552 | bytes 4726784 | tf_op jit(solution)/shard_map/fqn,bncp->fbqcp/dot_general | solution.py:40
  75.9 1.5 %copy.40 = f32[8,1,2,3,4096]{4,2,3,1,0:T(2,128)} copy(f32[8,1,2,3,4096]{4,0,3,2,1:T(8,128)S(1)} %fusion) | data formatting | bytes 1572864 | tf_op jit(solution)/shard_map/add | solution.py:50
  77.4 6.3 %all-to-all-start = ((f32[8,1,2,3,4096]{4,2,3,1,0:T(2,128)}), f32[8,1,2,3,4096]{4,2,3,1,0:T(2,128)S(1)}, u32[]{:S(2)}, u32[]{:S(2)}) async-start(f32[8,1,2,3,4096]{4,2,3,1,0:T(2,128)} %copy.40), calls=%async_computation | async-start | bytes 1572864 | tf_op jit(solution)/shard_map/all_to_all | solution.py:53
  83.8 0.0 copy-done
  83.8 19.4 %all-to-all-done = f32[8,1,2,3,4096]{4,2,3,1,0:T(2,128)S(1)} async-done(((f32[8,1,2,3,4096]{4,2,3,1,0:T(2,128)}), f32[8,1,2,3,4096]{4,2,3,1,0:T(2,128)S(1)}, u32[]{:S(2)}, u32[]{:S(2)}) %all-to-all-start) | async-done | bytes 786464 | tf_op jit(solution)/shard_map/all_to_all | solution.py:53
  103.2 0.3 multiply_bitcast_fusion
  103.5 5.3 %convolution_bitcast_fusion = f32[1,8,2,8,2]{3,1,4,2,0:T(8,128)S(1)} fusion(f32[8,2,3,4096,1]{3,1,2,0,4:T(2,128)S(1)} %multiply_bitcast_fusion, f32[8,1,2,3,4096]{4,2,3,1,0:T(2,128)S(1)} %all-to-all-done), kind=kOutput, calls=%fused_computation.7 | convolution fusion | flops 37748736 | bytes 1573888 | tf_op jit(solution)/shard_map/fir,fjr->fij/dot_general | solution.py:61
  108.8 0.2 copy.59
  109.0 0.1 reshape.299
  109.1 5.8 %psum.7 = f32[1,16,16]{1,2,0:T(8,128)S(1)} all-reduce(f32[1,16,16]{1,2,0:T(8,128)S(1)} %reshape.299), channel_id=1, replica_groups=mesh['freq'=8,'space'=4] {'space'}, use_global_device_ids=true, to_apply=%region_1.2 | all-reduce | flops 256 | bytes 2048 | tf_op jit(solution)/shard_map/psum | solution.py:63
  114.8 0.1 copy.45
  114.9 1.5 %custom-call.7 = f32[1,16,16]{2,1,0:T(8,128)S(1)} custom-call(f32[1,16,16]{2,1,0:T(8,128)S(1)} %fusion.10), custom_call_target="Cholesky" | custom-call | tf_op jit(solution)/shard_map/jit(cholesky)/cholesky | solution.py:63
  116.4 0.6 compare_reduce_fusion
  117.0 0.6 fusion.11
  117.7 0.1 copy.50
  117.8 0.1 reshape.289
  117.9 0.1 slice_reduce_fusion.1
  118.0 1.2 %custom-call.8 = f32[1,1,16,16]{2,3,1,0:T(8,128)S(1)} custom-call(f32[1,1,16,16]{3,2,1,0:T(8,128)S(1)} %get-tuple-element.17), custom_call_target="InvertDiagBlocksLowerTriangular" | custom-call | tf_op jit(solution)/shard_map/triangular_solve | solution.py:64
  119.2 0.1 copy.46
  119.3 0.6 copy.47
  119.9 1.1 fusion.1
  121.0 1.2 copy.51
  122.2 0.6 pad_maximum_fusion.1
  (9 shorter events, 0.1 us)
Async XLA Ops:
  0.6 73.7 %collective-permute-start = (f32[64,3,4096]{2,0,1:T(8,128)}, f32[64,3,4096]{2,0,1:T(8,128)S(1)}, u32[]{:S(2)}, u32[]{:S(2)}) collective-permute-start(f32[64,3,4096]{2,0,1:T(8,128)} %param.3), channel_id=1, source_target_pairs={{0,28},{4,0},{8,4},{12,8},{16,12},{20,16},{24,20},{28,24},{1,29},{... | collective-permute-start | bytes 9437192 | tf_op jit(solution)/shard_map/ppermute | solution.py:15
  12.3 71.5 %copy-start = (f32[4096]{0:T(1024)S(1)}, f32[4096]{0:T(1024)}, u32[]{:S(2)}) copy-start(f32[4096]{0:T(1024)} %param.4) | copy-start | bytes 49156
  77.4 25.7 %all-to-all-start = ((f32[8,1,2,3,4096]{4,2,3,1,0:T(2,128)}), f32[8,1,2,3,4096]{4,2,3,1,0:T(2,128)S(1)}, u32[]{:S(2)}, u32[]{:S(2)}) async-start(f32[8,1,2,3,4096]{4,2,3,1,0:T(2,128)} %copy.40), calls=%async_computation | async-start | bytes 1572864 | tf_op jit(solution)/shard_map/all_to_all | solution.py:53
where the time goes:
time: 123 us
  waiting for transfers between devices  81.3 us (66%)
  starting transfers between devices  12.4 us (10%)
  matrix products  11.5 us (9%)
  other arithmetic  6.47 us (5%)
  blocking collectives  5.75 us (5%)
  local copies, waits for them, and re-layouts  3.89 us (3%)
  between operations  1.44 us (1%)
    ppermute x1, waiting for transfers between devices, shifted(): return lax.ppermute(value, axis, pairs)  62 us
    all_to_all x1, waiting for transfers between devices, per_device(): lax.all_to_all(spectra, 'freq', split_axis=0, concat_axis=1, tiled=True)  19.4 us
    all_to_all x1, starting transfers between devices, per_device(): lax.all_to_all(spectra, 'freq', split_axis=0, concat_axis=1, tiled=True)  6.35 us
    ppermute x1, starting transfers between devices, shifted(): return lax.ppermute(value, axis, pairs)  6.03 us
    psum x1, blocking collectives, per_device(): lower_factor = jnp.linalg.cholesky(lax.psum(local_gram, 'space'))  5.75 us
    dot_general x1, matrix products, per_device(): jnp.einsum('fir,fjr->fij', weighted, flattened, precision=lax.Precision.H...  5.27 us
    dot_general x2, matrix products, apply_table(): jnp.einsum('fqn,bncp->fbqcp', transform, groups, precision=lax.Precision....  5.1 us
  transfers between devices with their start and end apart: 2, of which 2 were waited for; matrix products, arithmetic and copies ran while one was open for 4% of the time, Pallas kernels for 0%

commit v1 on v0

v1 whole, which is shorter than its diff:
```python
import functools
import math

import jax
import jax.numpy as jnp
from jax import lax
from jax.experimental import pallas as pl
from jax.experimental.pallas import tpu as pltpu
from jax.sharding import PartitionSpec as P

PTS = 16384
SAMPLES = 128
HALF = SAMPLES // 2
COMPS = 3
CUTS = 2
F32, BF16 = jnp.float32, jnp.bfloat16
MESH = pl.DeviceIdType.MESH


def split3(value):
    first = value.astype(BF16)
    rest = value - first.astype(F32)
    second = rest.astype(BF16)
    third = (rest - second.astype(F32)).astype(BF16)
    return first, second, third


def turn(steps):
    shifted = (steps + 16) & 127
    quarter = shifted >> 5
    small = ((shifted & 31) - 16).astype(F32) * (math.pi / 64.0)
    square = small * small
    sine = small * (1.0 + square * (-1.0 / 6 + square * (1.0 / 120 + square * (-1.0 / 5040 + square * (1.0 / 362880)))))
    cosine = 1.0 + square * (-0.5 + square * (1.0 / 24 + square * (-1.0 / 720 + square * (1.0 / 40320 - square * (1.0 / 3628800)))))
    odd = (quarter & 1) == 1
    cos_size, sin_size = jnp.where(odd, sine, cosine), jnp.where(odd, cosine, sine)
    cos_value = jnp.where((quarter == 1) | (quarter == 2), -cos_size, cos_size)
    sin_value = jnp.where(quarter >= 2, -sin_size, sin_size)
    return cos_value, sin_value


def build_table(bins_ref, pairs, me_x):
    rows = 8 * pairs
    row = lax.broadcasted_iota(jnp.int32, (rows, HALF), 0)
    sample = lax.broadcasted_iota(jnp.int32, (rows, HALF), 1)
    bin_value = jnp.zeros((rows, HALF), jnp.int32)
    for group in range(2):
        parity = me_x if group == 0 else 1 - me_x
        for other in range(pairs):
            value = bins_ref[2 * other + parity]
            here = ((row // (4 * pairs)) == group) & (((row % (2 * pairs)) // 2) == other)
            bin_value = jnp.where(here, value, bin_value)
    trailing = ((row // (2 * pairs)) + me_x) & 1
    sample = sample + HALF * trailing
    cosine, sine = turn((bin_value * sample) & 127)
    window_cos, _ = turn(sample)
    window = (0.5 - 0.5 * window_cos) * (1.0 / math.sqrt(48.0))
    return jnp.where((row & 1) == 0, cosine, -sine) * window


def kernel(pairs, spaces, bins_ref, weight_ref, record_ref, modes_ref, factor_ref,
           rec, wbuf, xsend, xrecv, abuf, zsend, zrecv, split, gsend, grecv,
           in_sem, w_sem, x_ssem, x_rsem, e_ssem, e_rsem, l_ssem, l_rsem, g_ssem, g_rsem):
    blocks = 2 * pairs
    two = 2 * blocks
    points = record_ref.shape[2]
    cols = points // CUTS
    chunks = COMPS * CUTS
    me = lax.axis_index("freq")
    my_s = lax.axis_index("space")
    me_x = lax.rem(me, 2)
    me_z = lax.div(me, 2)
    partner = me + 1 - 2 * me_x
    early = 2 - 2 * me_x
    late = 2 * me_x

    barrier = pltpu.get_barrier_semaphore()
    pl.semaphore_signal(barrier, inc=1, device_id=(partner, my_s), device_id_type=MESH)
    for step in range(1, pairs):
        pl.semaphore_signal(barrier, inc=1, device_id=(lax.rem(me + 2 * step, blocks), my_s), device_id_type=MESH)
    for step in range(1, spaces):
        pl.semaphore_signal(barrier, inc=1, device_id=(me, lax.rem(my_s + step, spaces)), device_id_type=MESH)

    loads = []
    for k in range(chunks):
        load = pltpu.make_async_copy(
            record_ref.at[k // CUTS, :, pl.ds((k % CUTS) * cols, cols)], rec.at[k], in_sem.at[k])
        load.start()
        loads.append(load)
    w_load = pltpu.make_async_copy(weight_ref, wbuf, w_sem)
    w_load.start()

    t1, t2, t3 = split3(build_table(bins_ref, pairs, me_x))
    table_a = jnp.concatenate([t1, t2, t1], axis=1)
    table_b = jnp.concatenate([t2, t3, t1], axis=1)

    pl.semaphore_wait(barrier, 1 + (pairs - 1) + (spaces - 1))

    sends = []
    xcopies = []
    for k in range(chunks):
        loads[k].wait()
        r1, r2, r3 = split3(rec[k])
        part = jnp.dot(table_a, jnp.concatenate([r1, r1, r2], axis=0), preferred_element_type=F32) + jnp.dot(
            table_b, jnp.concatenate([r2, r1, r3], axis=0), preferred_element_type=F32)
        xsend[k] = part[4 * pairs:]
        copy = pltpu.make_async_remote_copy(
            src_ref=xsend.at[k], dst_ref=xrecv.at[k], send_sem=x_ssem.at[k], recv_sem=x_rsem.at[k],
            device_id=(partner, my_s), device_id_type=MESH)
        copy.start()
        xcopies.append(copy)
        abuf[k] = part[:2 * pairs]
        for other in range(pairs):
            zsend[k, other, early] = part[2 * pairs + 2 * other:2 * pairs + 2 * other + 2]
        for step in range(1, pairs):
            to = lax.rem(me_z + step, pairs)
            copy = pltpu.make_async_remote_copy(
                src_ref=zsend.at[k, to, early], dst_ref=zrecv.at[k, me_z, early],
                send_sem=e_ssem.at[k, step], recv_sem=e_rsem.at[k, step],
                device_id=(2 * to + me_x, my_s), device_id_type=MESH)
            copy.start()
            sends.append(copy)

    for k in range(chunks):
        xcopies[k].wait_recv()
        total = abuf[k] + xrecv[k, :2 * pairs]
        passed = xrecv[k, 2 * pairs:]
        for other in range(pairs):
            zsend[k, other, 1] = total[2 * other:2 * other + 2]
            zsend[k, other, late] = passed[2 * other:2 * other + 2]
        for step in range(1, pairs):
            to = lax.rem(me_z + step, pairs)
            copy = pltpu.make_async_remote_copy(
                src_ref=zsend.at[k, to, pl.ds(me_x, 2)], dst_ref=zrecv.at[k, me_z, pl.ds(me_x, 2)],
                send_sem=l_ssem.at[k, step], recv_sem=l_rsem.at[k, step],
                device_id=(2 * to + me_x, my_s), device_id_type=MESH)
            copy.start()
            sends.append(copy)
        zrecv[k, me_z] = zsend[k, me_z]

    w_load.wait()
    gram = None
    per = 2 * (pairs - 1)
    for k in range(chunks):
        comp, cut = k // CUTS, k % CUTS
        for step in range(1, pairs):
            sends[k * (pairs - 1) + step - 1].wait_recv()
            sends[(chunks + k) * (pairs - 1) + step - 1].wait_recv()
        pieces = []
        for z in range(pairs):
            pieces.append(zrecv[k, z, 1])
            pieces.append(zrecv[k, z, 0] + zrecv[k, (z + 1) % pairs, 2])
        value = jnp.concatenate([piece[0:1] for piece in pieces] + [piece[1:2] for piece in pieces], axis=0)
        parts = jnp.concatenate(split3(value), axis=0)
        split[comp, :, cut * cols:(cut + 1) * cols] = parts
        weighted = value * (wbuf[:, cut * cols:(cut + 1) * cols] * (1.0 / (COMPS * PTS)))
        wparts = jnp.concatenate(split3(weighted), axis=0)
        product = lax.dot_general(wparts, parts, (((1,), (1,)), ((), ())), preferred_element_type=F32)
        gram = product if gram is None else gram + product
    small = None
    for i in (2, 1, 0):
        for j in (2, 1, 0):
            term = gram[i * two:(i + 1) * two, j * two:(j + 1) * two]
            small = term if small is None else small + term
    real = small[:blocks, :blocks] + small[blocks:, blocks:]
    imag = small[:blocks, blocks:] - small[blocks:, :blocks]
    gsend[...] = jnp.concatenate([real, imag] + [jnp.zeros((blocks, gsend.shape[1] - two), F32)] * (gsend.shape[1] > two), axis=1)
    gcopies = []
    for step in range(1, spaces):
        copy = pltpu.make_async_remote_copy(
            src_ref=gsend, dst_ref=grecv.at[my_s], send_sem=g_ssem.at[step], recv_sem=g_rsem.at[step],
            device_id=(me, lax.rem(my_s + step, spaces)), device_id_type=MESH)
        copy.start()
        gcopies.append(copy)
    grecv[my_s] = gsend[...]
    for copy in gcopies:
        copy.wait_recv()
    whole = grecv[0]
    for s in range(1, spaces):
        whole = whole + grecv[s]

    row = lax.broadcasted_iota(jnp.int32, (blocks, two), 0)
    lane = lax.broadcasted_iota(jnp.int32, (blocks, two), 1)
    unit = (lane == row + blocks).astype(F32)
    left = lane < blocks
    re = jnp.where(left, whole[:, :two], unit)
    im = jnp.where(left, jnp.concatenate([whole[:, blocks:two], whole[:, :blocks]], axis=1), 0.0)
    for j in range(blocks - 1):
        inverse = 1.0 / re[j:j + 1, j:j + 1]
        row_re, row_im = re[j:j + 1] * inverse, im[j:j + 1] * inverse
        below = row > j
        col_re = jnp.where(below, re[:, j:j + 1], 0.0)
        col_im = jnp.where(below, im[:, j:j + 1], 0.0)
        re, im = re - (col_re * row_re - col_im * row_im), im - (col_re * row_im + col_im * row_re)
    pivots = jnp.sum(jnp.where(lane == row, re, 0.0), axis=1, keepdims=True)
    scale = 1.0 / jnp.sqrt(pivots)
    re, im = re * scale, im * scale
    factor_ref[0] = jnp.where(lane >= row, re, 0.0)[:, :blocks]
    factor_ref[1] = jnp.where(lane > row, im, 0.0)[:, :blocks]
    wr, wi = re[:, blocks:], im[:, blocks:]
    upper = jnp.concatenate([wr, wi], axis=1)
    lower = jnp.concatenate([-wi, wr], axis=1)
    mixed = jnp.concatenate([src[b:b + 1] for b in range(blocks) for src in (upper, lower)], axis=0)
    m1, m2, m3 = split3(mixed)
    weights = jnp.concatenate([m1, m1, m2, m2, m1, m3], axis=1)
    for comp in range(COMPS):
        x1, x2, x3 = (split[comp, i * two:(i + 1) * two] for i in range(3))
        out = jnp.dot(weights, jnp.concatenate([x1, x2, x1, x2, x3, x1], axis=0), preferred_element_type=F32)
        modes_ref[comp] = out.astype(BF16)
    for copy in xcopies + sends + gcopies:
        copy.wait_send()


def solution(mesh):
    count, spaces = mesh.shape["freq"], mesh.shape["space"]
    pairs = count // 2

    def per_device(record, area_weight, freq_bins):
        points = record.shape[2]
        cols = points // CUTS
        chunks = COMPS * CUTS
        two = 2 * count
        lanes = max(128, two)
        dma = pltpu.SemaphoreType.DMA
        modes, factor = pl.pallas_call(
            functools.partial(kernel, pairs, spaces),
            out_shape=(
                jax.ShapeDtypeStruct((COMPS, two, points), BF16),
                jax.ShapeDtypeStruct((2, count, count), F32),
            ),
            in_specs=[
                pl.BlockSpec(memory_space=pltpu.SMEM),
                pl.BlockSpec(memory_space=pl.ANY),
                pl.BlockSpec(memory_space=pl.ANY),
            ],
            out_specs=(pl.BlockSpec(memory_space=pltpu.VMEM), pl.BlockSpec(memory_space=pltpu.VMEM)),
            scratch_shapes=[
                pltpu.VMEM((chunks, HALF, cols), F32),
                pltpu.VMEM((1, points), F32),
                pltpu.VMEM((chunks, 4 * pairs, cols), F32),
                pltpu.VMEM((chunks, 4 * pairs, cols), F32),
                pltpu.VMEM((chunks, 2 * pairs, cols), F32),
                pltpu.VMEM((chunks, pairs, 3, 2, cols), F32),
                pltpu.VMEM((chunks, pairs, 3, 2, cols), F32),
                pltpu.VMEM((COMPS, 3 * two, points), BF16),
                pltpu.VMEM((count, lanes), F32),
                pltpu.VMEM((spaces, count, lanes), F32),
                dma((chunks,)), dma,
                dma((chunks,)), dma((chunks,)),
                dma((chunks, pairs)), dma((chunks, pairs)),
                dma((chunks, pairs)), dma((chunks, pairs)),
                dma((spaces,)), dma((spaces,)),
            ],
            compiler_params=pltpu.CompilerParams(
                collective_id=0, has_side_effects=True, vmem_limit_bytes=56 * 1024 * 1024),
        )(freq_bins, area_weight.reshape(1, points), record.transpose(1, 0, 2))
        modes = modes.reshape(COMPS, count, 2, points).transpose(1, 2, 0, 3)
        return modes[None], factor[None]

    return jax.shard_map(
        per_device,
        mesh=mesh,
        in_specs=(P("freq", None, "space"), P("space"), P()),
        out_specs=(P("freq", None, None, None, "space"), P("freq", None, None, None)),
        check_vma=False,
    )
```

time: 123 us -> 43.8 us (0.36)
  waiting for transfers between devices: 81.3 us -> 0 us
  Pallas kernels: 0 us -> 39.3 us
  starting transfers between devices: 12.4 us -> 0 us
  matrix products: 11.5 us -> 0 us
  other arithmetic: 6.47 us -> 0 us
  blocking collectives: 5.75 us -> 0 us
    ppermute x1 -> x0, waiting for transfers between devices: 62 us -> none  [shifted(): return lax.ppermute(value, axis, pairs)]
    pallas_call x0 -> x1, Pallas kernels: none -> 39.3 us  [per_device(): pl.pallas_call(functools.partial(kernel, pairs, spaces), out_shape=(jax.S...]
    all_to_all x1 -> x0, waiting for transfers between devices: 19.4 us -> none  [per_device(): lax.all_to_all(spectra, 'freq', split_axis=0, concat_axis=1, tiled=True)]
    dot_general x3 -> x0, matrix products: 10.4 us -> none  [the longest x1 5.27 us: per_device(): jnp.einsum('fir,fjr->fij', weighted, flattened, precision=lax.Precision.H...]
    all_to_all x1 -> x0, starting transfers between devices: 6.35 us -> none  [per_device(): lax.all_to_all(spectra, 'freq', split_axis=0, concat_axis=1, tiled=True)]
    ppermute x1 -> x0, starting transfers between devices: 6.03 us -> none  [shifted(): return lax.ppermute(value, axis, pairs)]
    psum x1 -> x0, blocking collectives: 5.75 us -> none  [per_device(): lower_factor = jnp.linalg.cholesky(lax.psum(local_gram, 'space'))]
    another operation x8 -> x0, other arithmetic: 4.31 us -> none  [the longest x3 2.13 us: per_device(): lower_factor = jnp.linalg.cholesky(lax.psum(local_gram, 'space'))]
  transfers between devices with their start and end apart: 2 -> 0, of which waited for: 2 -> 0; matrix products, arithmetic and copies ran while one was open for 4% -> 0% of each run, Pallas kernels for 0% -> 0%
where the time goes in v1:
time: 43.8 us; the launch traced here: 43.6 us
  Pallas kernels  39.3 us (90%)
  local copies, waits for them, and re-layouts  3.64 us (8%)
  between operations  0.64 us (1%)
    pallas_call x1, Pallas kernels, per_device(): pl.pallas_call(functools.partial(kernel, pairs, spaces), out_shape=(jax.S...  39.3 us
    reshape x2, local copies, waits for them, and re-layouts, per_device(): modes = modes.reshape(COMPS, count, 2, points).transpose(1, 2, 0, 3)  2.35 us
    unnamed x1, local copies, waits for them, and re-layouts  1.29 us

profile of v1, /device:TPU:0, one launch (start us, length us, event | category | flops | bytes accessed | tf_op | source)
XLA Modules:
  0.0 43.6 jit_solution(9829932100194868372)
XLA Ops:
  0.6 39.3 %shard_map.50 = (bf16[3,16,4096]{2,1,0:T(8,128)(2,1)}, f32[2,8,8]{2,1,0:T(8,128)}) custom-call(s32[8]{0:T(128)} %bins_ref.1, f32[1,4096]{1,0:T(1,128)} %bitcast.10, f32[3,64,4096]{2,1,0:T(8,128)} %bitcast.8), custom_call_target="tpu_custom_call" | custom-call | tf_op jit(solution)/shard_map/pallas_call | solution.py:225
  39.9 1.3 %reshape.11 = bf16[3,8,2,4096]{3,2,1,0:T(2,128)(2,1)S(1)} reshape(bf16[3,16,4096]{2,1,0:T(8,128)(2,1)} %get-tuple-element.4) | data formatting | bytes 786432 | tf_op jit(solution)/shard_map/reshape | solution.py:257
  41.2 1.1 %copy.7 = bf16[3,8,2,4096]{3,2,0,1:T(2,128)(2,1)} copy(bf16[3,8,2,4096]{3,2,1,0:T(2,128)(2,1)S(1)} %reshape.11) | data formatting | bytes 786432 | tf_op jit(solution)/shard_map/reshape | solution.py:257
  42.3 1.3 %copy.9 = f32[1,2,8,8]{3,2,1,0:T(8,128)} copy(f32[1,2,8,8]{3,2,1,0:T(8,128)} %bitcast.11) | data formatting | bytes 1024

commit v2 on v1

--- a/solution.py
+++ b/solution.py
@@ -58,9 +58,9 @@
     return jnp.where((row & 1) == 0, cosine, -sine) * window
 
 
-def kernel(pairs, spaces, bins_ref, weight_ref, record_ref, modes_ref, factor_ref,
+def kernel(pairs, spaces, bins_ref, weight_ref, record_ref, split_ref, gram_ref,
            rec, wbuf, xsend, xrecv, abuf, zsend, zrecv, split, gsend, grecv,
-           in_sem, w_sem, x_ssem, x_rsem, e_ssem, e_rsem, l_ssem, l_rsem, g_ssem, g_rsem):
+           in_sem, w_sem, out_sem, x_ssem, x_rsem, e_ssem, e_rsem, l_ssem, l_rsem, g_ssem, g_rsem):
     blocks = 2 * pairs
     two = 2 * blocks
     points = record_ref.shape[2]
@@ -140,6 +140,7 @@
 
     w_load.wait()
     gram = None
+    stores = []
     per = 2 * (pairs - 1)
     for k in range(chunks):
         comp, cut = k // CUTS, k % CUTS
@@ -152,7 +153,11 @@
             pieces.append(zrecv[k, z, 0] + zrecv[k, (z + 1) % pairs, 2])
         value = jnp.concatenate([piece[0:1] for piece in pieces] + [piece[1:2] for piece in pieces], axis=0)
         parts = jnp.concatenate(split3(value), axis=0)
-        split[comp, :, cut * cols:(cut + 1) * cols] = parts
+        split[k] = parts
+        store = pltpu.make_async_copy(
+            split.at[k], split_ref.at[comp, :, pl.ds(cut * cols, cols)], out_sem.at[k])
+        store.start()
+        stores.append(store)
         weighted = value * (wbuf[:, cut * cols:(cut + 1) * cols] * (1.0 / (COMPS * PTS)))
         wparts = jnp.concatenate(split3(weighted), axis=0)
         product = lax.dot_general(wparts, parts, (((1,), (1,)), ((), ())), preferred_element_type=F32)
@@ -179,6 +184,21 @@
     for s in range(1, spaces):
         whole = whole + grecv[s]
 
+    gram_ref[...] = whole
+    for copy in stores:
+        copy.wait()
+    for copy in xcopies + sends + gcopies:
+        copy.wait_send()
+
+
+def finish(blocks, gram_ref, split_ref, modes_ref, factor_ref, held, sem):
+    two = 2 * blocks
+    loads = []
+    for comp in range(COMPS):
+        load = pltpu.make_async_copy(split_ref.at[comp], held.at[comp], sem.at[comp])
+        load.start()
+        loads.append(load)
+    whole = gram_ref[...]
     row = lax.broadcasted_iota(jnp.int32, (blocks, two), 0)
     lane = lax.broadcasted_iota(jnp.int32, (blocks, two), 1)
     unit = (lane == row + blocks).astype(F32)
@@ -204,11 +224,11 @@
     m1, m2, m3 = split3(mixed)
     weights = jnp.concatenate([m1, m1, m2, m2, m1, m3], axis=1)
     for comp in range(COMPS):
-        x1, x2, x3 = (split[comp, i * two:(i + 1) * two] for i in range(3))
+        loads[comp].wait()
+        x1, x2, x3 = (held[comp, i * two:(i + 1) * two] for i in range(3))
         out = jnp.dot(weights, jnp.concatenate([x1, x2, x1, x2, x3, x1], axis=0), preferred_element_type=F32)
-        modes_ref[comp] = out.astype(BF16)
-    for copy in xcopies + sends + gcopies:
-        copy.wait_send()
+        for b in range(blocks):
+            modes_ref[b, comp] = out[2 * b:2 * b + 2].astype(BF16)
 
 
 def solution(mesh):
@@ -222,18 +242,18 @@
         two = 2 * count
         lanes = max(128, two)
         dma = pltpu.SemaphoreType.DMA
-        modes, factor = pl.pallas_call(
+        split, gram = pl.pallas_call(
             functools.partial(kernel, pairs, spaces),
             out_shape=(
-                jax.ShapeDtypeStruct((COMPS, two, points), BF16),
-                jax.ShapeDtypeStruct((2, count, count), F32),
+                jax.ShapeDtypeStruct((COMPS, 3 * two, points), BF16),
+                jax.ShapeDtypeStruct((count, lanes), F32),
             ),
             in_specs=[
                 pl.BlockSpec(memory_space=pltpu.SMEM),
                 pl.BlockSpec(memory_space=pl.ANY),
                 pl.BlockSpec(memory_space=pl.ANY),
             ],
-            out_specs=(pl.BlockSpec(memory_space=pltpu.VMEM), pl.BlockSpec(memory_space=pltpu.VMEM)),
+            out_specs=(pl.BlockSpec(memory_space=pl.ANY), pl.BlockSpec(memory_space=pltpu.VMEM)),
             scratch_shapes=[
                 pltpu.VMEM((chunks, HALF, cols), F32),
                 pltpu.VMEM((1, points), F32),
@@ -242,10 +262,10 @@
                 pltpu.VMEM((chunks, 2 * pairs, cols), F32),
                 pltpu.VMEM((chunks, pairs, 3, 2, cols), F32),
                 pltpu.VMEM((chunks, pairs, 3, 2, cols), F32),
-                pltpu.VMEM((COMPS, 3 * two, points), BF16),
+                pltpu.VMEM((chunks, 3 * two, cols), BF16),
                 pltpu.VMEM((count, lanes), F32),
                 pltpu.VMEM((spaces, count, lanes), F32),
-                dma((chunks,)), dma,
+                dma((chunks,)), dma, dma((chunks,)),
                 dma((chunks,)), dma((chunks,)),
                 dma((chunks, pairs)), dma((chunks, pairs)),
                 dma((chunks, pairs)), dma((chunks, pairs)),
@@ -254,8 +274,18 @@
             compiler_params=pltpu.CompilerParams(
                 collective_id=0, has_side_effects=True, vmem_limit_bytes=56 * 1024 * 1024),
         )(freq_bins, area_weight.reshape(1, points), record.transpose(1, 0, 2))
-        modes = modes.reshape(COMPS, count, 2, points).transpose(1, 2, 0, 3)
-        return modes[None], factor[None]
+        modes, factor = pl.pallas_call(
+            functools.partial(finish, count),
+            out_shape=(
+                jax.ShapeDtypeStruct((count, COMPS, 2, points), BF16),
+                jax.ShapeDtypeStruct((2, count, count), F32),
+            ),
+            in_specs=[pl.BlockSpec(memory_space=pltpu.VMEM), pl.BlockSpec(memory_space=pl.ANY)],
+            out_specs=(pl.BlockSpec(memory_space=pltpu.VMEM), pl.BlockSpec(memory_space=pltpu.VMEM)),
+            scratch_shapes=[pltpu.VMEM((COMPS, 3 * two, points), BF16), dma((COMPS,))],
+            compiler_params=pltpu.CompilerParams(vmem_limit_bytes=56 * 1024 * 1024),
+        )(gram, split)
+        return modes.transpose(0, 2, 1, 3)[None], factor[None]
 
     return jax.shard_map(
         per_device,

time: 43.8 us -> 41.7 us (0.952)
  local copies, waits for them, and re-layouts: 3.64 us -> 0 us
  Pallas kernels: 39.3 us -> 40.9 us
    pallas_call x0 -> x1, Pallas kernels: none -> 3.13 us  [per_device(): pl.pallas_call(functools.partial(finish, count), out_shape=(jax.ShapeDtyp...]
    reshape x2 -> x0, local copies, waits for them, and re-layouts: 2.35 us -> none  [per_device(): modes = modes.reshape(COMPS, count, 2, points).transpose(1, 2, 0, 3)]
    pallas_call x1, Pallas kernels: 39.3 us -> 37.8 us  [per_device(): pl.pallas_call(functools.partial(kernel, pairs, spaces), out_shape=(jax.S...]
    unnamed x1 -> x0, local copies, waits for them, and re-layouts: 1.29 us -> none
where the time goes in v2:
time: 41.7 us; the launch traced here: 41.6 us
  Pallas kernels  40.9 us (98%)
  between operations  0.64 us (2%)
    pallas_call x1, Pallas kernels, per_device(): pl.pallas_call(functools.partial(kernel, pairs, spaces), out_shape=(jax.S...  37.8 us
    pallas_call x1, Pallas kernels, per_device(): pl.pallas_call(functools.partial(finish, count), out_shape=(jax.ShapeDtyp...  3.13 us

profile of v2, /device:TPU:0, one launch (start us, length us, event | category | flops | bytes accessed | tf_op | source)
XLA Modules:
  0.0 41.6 jit_solution(15119643506259524957)
XLA Ops:
  0.6 37.8 %shard_map.50 = (bf16[3,48,4096]{2,1,0:T(8,128)(2,1)}, f32[8,128]{1,0:T(8,128)}) custom-call(s32[8]{0:T(128)} %bins_ref.1, f32[1,4096]{1,0:T(1,128)} %bitcast.7, f32[3,64,4096]{2,1,0:T(8,128)} %bitcast.6), custom_call_target="tpu_custom_call" | custom-call | tf_op jit(solution)/shard_map/pallas_call | solution.py:245
  38.4 3.1 %shard_map.51 = (bf16[8,3,2,4096]{3,2,1,0:T(2,128)(2,1)}, f32[2,8,8]{2,1,0:T(8,128)}) custom-call(f32[8,128]{1,0:T(8,128)} %get-tuple-element.6.gram_ref, bf16[3,48,4096]{2,1,0:T(8,128)(2,1)} %get-tuple-element.7.split_ref), custom_call_target="tpu_custom_call" | custom-call | tf_op jit(solution)/shard_map/pallas_call | solution.py:277

commit v3 on v2

--- a/solution.py
+++ b/solution.py
@@ -162,11 +162,8 @@
         wparts = jnp.concatenate(split3(weighted), axis=0)
         product = lax.dot_general(wparts, parts, (((1,), (1,)), ((), ())), preferred_element_type=F32)
         gram = product if gram is None else gram + product
-    small = None
-    for i in (2, 1, 0):
-        for j in (2, 1, 0):
-            term = gram[i * two:(i + 1) * two, j * two:(j + 1) * two]
-            small = term if small is None else small + term
+    tall = (gram[2 * two:] + gram[two:2 * two]) + gram[:two]
+    small = (tall[:, 2 * two:] + tall[:, two:2 * two]) + tall[:, :two]
     real = small[:blocks, :blocks] + small[blocks:, blocks:]
     imag = small[:blocks, blocks:] - small[blocks:, :blocks]
     gsend[...] = jnp.concatenate([real, imag] + [jnp.zeros((blocks, gsend.shape[1] - two), F32)] * (gsend.shape[1] > two), axis=1)
@@ -178,6 +175,10 @@
         copy.start()
         gcopies.append(copy)
     grecv[my_s] = gsend[...]
+    for copy in stores:
+        copy.wait()
+    for copy in xcopies + sends:
+        copy.wait_send()
     for copy in gcopies:
         copy.wait_recv()
     whole = grecv[0]
@@ -185,9 +186,7 @@
         whole = whole + grecv[s]
 
     gram_ref[...] = whole
-    for copy in stores:
-        copy.wait()
-    for copy in xcopies + sends + gcopies:
+    for copy in gcopies:
         copy.wait_send()
 
 

time: 41.7 us -> 41.7 us (level)
  no operation moved by 1% of the time
where the time goes in v3:
time: 41.7 us; the launch traced here: 41.5 us
  Pallas kernels  40.9 us (98%)
  between operations  0.64 us (2%)
    pallas_call x1, Pallas kernels, per_device(): pl.pallas_call(functools.partial(kernel, pairs, spaces), out_shape=(jax.S...  37.8 us
    pallas_call x1, Pallas kernels, per_device(): pl.pallas_call(functools.partial(finish, count), out_shape=(jax.ShapeDtyp...  3.13 us

profile of v3, /device:TPU:0, one launch (start us, length us, event | category | flops | bytes accessed | tf_op | source)
XLA Modules:
  0.0 41.5 jit_solution(15116602040856585263)
XLA Ops:
  0.6 37.8 %shard_map.50 = (bf16[3,48,4096]{2,1,0:T(8,128)(2,1)}, f32[8,128]{1,0:T(8,128)}) custom-call(s32[8]{0:T(128)} %bins_ref.1, f32[1,4096]{1,0:T(1,128)} %bitcast.7, f32[3,64,4096]{2,1,0:T(8,128)} %bitcast.6), custom_call_target="tpu_custom_call" | custom-call | tf_op jit(solution)/shard_map/pallas_call | solution.py:244
  38.4 3.1 %shard_map.51 = (bf16[8,3,2,4096]{3,2,1,0:T(2,128)(2,1)}, f32[2,8,8]{2,1,0:T(8,128)}) custom-call(f32[8,128]{1,0:T(8,128)} %get-tuple-element.6.gram_ref, bf16[3,48,4096]{2,1,0:T(8,128)(2,1)} %get-tuple-element.7.split_ref), custom_call_target="tpu_custom_call" | custom-call | tf_op jit(solution)/shard_map/pallas_call | solution.py:276

commit v4 on v3

--- a/solution.py
+++ b/solution.py
@@ -112,7 +112,7 @@
         abuf[k] = part[:2 * pairs]
         for other in range(pairs):
             zsend[k, other, early] = part[2 * pairs + 2 * other:2 * pairs + 2 * other + 2]
-        for step in range(1, pairs):
+        for step in sorted(range(1, pairs), key=lambda step: abs(step - pairs // 2)):
             to = lax.rem(me_z + step, pairs)
             copy = pltpu.make_async_remote_copy(
                 src_ref=zsend.at[k, to, early], dst_ref=zrecv.at[k, me_z, early],
@@ -128,7 +128,7 @@
         for other in range(pairs):
             zsend[k, other, 1] = total[2 * other:2 * other + 2]
             zsend[k, other, late] = passed[2 * other:2 * other + 2]
-        for step in range(1, pairs):
+        for step in sorted(range(1, pairs), key=lambda step: abs(step - pairs // 2)):
             to = lax.rem(me_z + step, pairs)
             copy = pltpu.make_async_remote_copy(
                 src_ref=zsend.at[k, to, pl.ds(me_x, 2)], dst_ref=zrecv.at[k, me_z, pl.ds(me_x, 2)],

time: 41.7 us -> 41.7 us (level)
  no operation moved by 1% of the time
where the time goes in v4:
time: 41.7 us; the launch traced here: 41.5 us
  Pallas kernels  40.9 us (98%)
  between operations  0.64 us (2%)
    pallas_call x1, Pallas kernels, per_device(): pl.pallas_call(functools.partial(kernel, pairs, spaces), out_shape=(jax.S...  37.8 us
    pallas_call x1, Pallas kernels, per_device(): pl.pallas_call(functools.partial(finish, count), out_shape=(jax.ShapeDtyp...  3.13 us

profile of v4, /device:TPU:0, one launch (start us, length us, event | category | flops | bytes accessed | tf_op | source)
XLA Modules:
  0.0 41.5 jit_solution(8982418603050015860)
XLA Ops:
  0.6 37.8 %shard_map.50 = (bf16[3,48,4096]{2,1,0:T(8,128)(2,1)}, f32[8,128]{1,0:T(8,128)}) custom-call(s32[8]{0:T(128)} %bins_ref.1, f32[1,4096]{1,0:T(1,128)} %bitcast.7, f32[3,64,4096]{2,1,0:T(8,128)} %bitcast.6), custom_call_target="tpu_custom_call" | custom-call | tf_op jit(solution)/shard_map/pallas_call | solution.py:244
  38.4 3.1 %shard_map.51 = (bf16[8,3,2,4096]{3,2,1,0:T(2,128)(2,1)}, f32[2,8,8]{2,1,0:T(8,128)}) custom-call(f32[8,128]{1,0:T(8,128)} %get-tuple-element.6.gram_ref, bf16[3,48,4096]{2,1,0:T(8,128)(2,1)} %get-tuple-element.7.split_ref), custom_call_target="tpu_custom_call" | custom-call | tf_op jit(solution)/shard_map/pallas_call | solution.py:276
